TPU v7x, 32 devices: a whole 2x2x4 slice. The times are simulated.
32 devices in a mesh: grp: 4 (over y, x), ep: 8 (over z, core).
Axes of the slice: x: 2, y: 2, z: 4, core: 2. Of those that a mesh axis runs over, the one named last changes fastest.
Arguments:
- tokens: bfloat16 [4096, 2048], P(('grp', 'ep')), may hold values from -6 to 6
- routes: int32 [4096, 6], P(('grp', 'ep')), may hold values from 0 to 7, all different within a row; in each aligned block of 128 rows (0 to 127, 128 to 255, ...) at most 128 rows name the same one
- route_gain: float32 [4096, 6], P(('grp', 'ep')), may hold values from 0.05 to 0.6
- gate_weight: bfloat16 [8, 2048, 768], P('ep', 'grp'), may hold values from -0.125 to 0.125
- up_weight: bfloat16 [8, 2048, 768], P('ep', 'grp'), may hold values from -0.125 to 0.125
- down_weight: bfloat16 [8, 768, 2048], P('ep', None, 'grp'), may hold values from -0.21875 to 0.21875
- norm_gain: float32 [2048], replicated, may hold values from 0.25 to 1.75
- query_weight: bfloat16 [2048, 1536], P(None, 'grp'), may hold values from -0.125 to 0.125
Outputs:
- mixed: bfloat16 [4096, 2048], P(('grp', 'ep'))
- query: bfloat16 [4096, 1536], P(('grp', 'ep'))
Inputs may be any that keep to these rules, and one draw needn't show every extreme that they name: `routes`: each row names 6 different experts. Among the 128 rows of one device no expert is named by more than 128 rows, a bound that some of them reach.
All inputs are finite; a program needn't handle non-finite values.
Results may differ from a plain program's by a relative error of at most 0.0053.
Values may be sent and summed in bfloat16 or wider, within the bound.
A program may use at most 128 MiB of HBM per device.

v0:
```python
import jax
import jax.numpy as jnp
from jax import lax
from jax.sharding import PartitionSpec as P


def shards(
    tokens, routes, route_gain, gate_weight, up_weight, down_weight, norm_gain, query_weight
):
    ep_count = lax.axis_size("ep")
    tok_rows = tokens.shape[0]
    width = tokens.shape[1]
    choose = routes.shape[1]
    capacity = 8 * tok_rows // ep_count
    flat = routes.reshape(-1)
    onehot = (flat[:, None] == jnp.arange(ep_count, dtype=jnp.int32)[None, :]).astype(jnp.int32)
    counted = jnp.cumsum(onehot, axis=0)
    rank = jnp.sum(onehot * (counted - 1), axis=1)
    slot = flat * capacity + rank
    repeated = jnp.repeat(tokens, choose, axis=0)
    outbound = jnp.zeros((ep_count * capacity, width), jnp.bfloat16).at[slot].set(repeated)
    arrived = lax.all_to_all(outbound, "ep", split_axis=0, concat_axis=0, tiled=True)
    gate = jnp.dot(
        arrived,
        lax.all_gather(gate_weight[0], "grp", axis=0, tiled=True),
        preferred_element_type=jnp.float32,
    )
    up = jnp.dot(
        arrived,
        lax.all_gather(up_weight[0], "grp", axis=0, tiled=True),
        preferred_element_type=jnp.float32,
    )
    hidden = (jax.nn.silu(gate) * up).astype(jnp.bfloat16)
    answers = jnp.dot(
        hidden,
        lax.all_gather(down_weight[0], "grp", axis=1, tiled=True),
        preferred_element_type=jnp.float32,
    ).astype(jnp.bfloat16)
    returned = lax.all_to_all(answers, "ep", split_axis=0, concat_axis=0, tiled=True)
    picked = returned[slot].reshape(tok_rows, choose, width).astype(jnp.float32)
    total = tokens.astype(jnp.float32) + jnp.sum(picked * route_gain[:, :, None], axis=1)
    square = jnp.mean(total * total, axis=-1, keepdims=True)
    normed = (total * lax.rsqrt(square + 1e-06) * norm_gain).astype(jnp.bfloat16)
    query = jnp.dot(
        normed,
        lax.all_gather(query_weight, "grp", axis=1, tiled=True),
        preferred_element_type=jnp.float32,
    ).astype(jnp.bfloat16)
    return (total.astype(jnp.bfloat16), query)


def solution(mesh):
    placed = (
        P(("grp", "ep"), None),
        P(("grp", "ep"), None),
        P(("grp", "ep"), None),
        P("ep", "grp", None),
        P("ep", "grp", None),
        P("ep", None, "grp"),
        P(),
        P(None, "grp"),
    )
    return jax.shard_map(
        shards,
        mesh=mesh,
        in_specs=placed,
        out_specs=(P(("grp", "ep"), None), P(("grp", "ep"), None)),
        check_vma=False,
    )
```

profile of v0, /device:TPU:0, one launch (start us, length us, event | category | flops | bytes accessed | tf_op | source)
XLA Modules:
  0.0 291.2 jit_solution(3708156401872762710)
XLA Ops:
  7.2 0.7 all-gather.12.cloned.1.call-update
  7.9 0.7 all-gather.10.cloned.1.call-update
  8.6 0.8 copy.14
  9.7 1.7 reduce-window.6
  11.7 0.2 reduce-window.9
  11.9 0.7 broadcast_multiply_fusion
  12.9 3.7 %broadcast_in_dim.5 = bf16[128,6,2048]{2,1,0:T(8,128)(2,1)} broadcast(bf16[128,2048]{1,0:T(8,128)(2,1)} %param.8), dimensions={0,2} | broadcast | bytes 3670016 | tf_op jit(solution)/shard_map/broadcast_in_dim | solution.py:20
  16.5 5.0 %reshape.87 = bf16[768,2048]{1,0:T(8,128)(2,1)S(1)} reshape(bf16[128,6,2048]{2,1,0:T(8,128)(2,1)} %broadcast_in_dim.5) | data formatting | bytes 6291456 | tf_op jit(solution)/shard_map/reshape | solution.py:20
  21.6 9.4 %scatter_custom_fusion = bf16[1024,2048]{1,0:T(8,128)(2,1)} fusion(s32[768]{0:T(1024)S(1)} %fusion.16, bf16[768,2048]{1,0:T(8,128)(2,1)S(1)} %reshape.87, bf16[]{:T(256)} %constant.9.clone.1), kind=kCustom, calls=%fused_computation.11 | custom fusion | bytes 4194306 | tf_op jit(solution)/shard_map/scatter | solution.py:21
  31.0 6.4 %all-to-all-start = ((bf16[8,128,2048]{2,1,0:T(8,128)(2,1)}), bf16[8,128,2048]{2,1,0:T(8,128)(2,1)}, u32[]{:S(2)}, u32[]{:S(2)}) async-start(bf16[8,128,2048]{2,1,0:T(8,128)(2,1)} %bitcast.28), calls=%async_computation | async-start | bytes 8388608 | tf_op jit(solution)/shard_map/all_to_all | solution.py:22
  37.4 0.7 all-gather.14.cloned.1.call-update
  38.2 0.5 all-gather.8.cloned.1.call-update
  38.7 17.9 %all-gather.12.cloned.1.call-done = bf16[1,2048,768]{2,1,0:T(8,128)(2,1)} async-done(((bf16[1,512,768]{2,1,0:T(8,128)(2,1)}), bf16[1,2048,768]{2,1,0:T(8,128)(2,1)}) %all-gather.12.cloned.1.call-update) | async-done | bytes 3145744 | tf_op jit(solution)/shard_map/all_gather | solution.py:30
  56.6 74.9 %all-to-all-done = bf16[8,128,2048]{2,1,0:T(8,128)(2,1)} async-done(((bf16[8,128,2048]{2,1,0:T(8,128)(2,1)}), bf16[8,128,2048]{2,1,0:T(8,128)(2,1)}, u32[]{:S(2)}, u32[]{:S(2)}) %all-to-all-start) | async-done | bytes 4194336 | tf_op jit(solution)/shard_map/all_to_all | solution.py:22
  131.5 6.2 %fusion.1 = f32[1024,768]{1,0:T(8,128)S(1)} fusion(bf16[1024,2048]{1,0:T(8,128)(2,1)} %bitcast.4, bf16[1,2048,768]{2,1,0:T(8,128)(2,1)} %all-gather.12.cloned.1.call-done), kind=kOutput, calls=%fused_computation.5 | convolution fusion | flops 3221225472 | bytes 10485760 | tf_op jit(solution)/shard_map/dot_general | solution.py:28
  137.8 10.4 %all-gather.14.cloned.1.call-done = bf16[1,768,2048]{2,1,0:T(8,128)(2,1)} async-done(((bf16[1,768,512]{2,1,0:T(8,128)(2,1)}), bf16[1,768,2048]{2,1,0:T(8,128)(2,1)}) %all-gather.14.cloned.1.call-update) | async-done | bytes 3145744 | tf_op jit(solution)/shard_map/all_gather | solution.py:36
  148.1 12.8 %convolution_convert_fusion = bf16[1024,2048]{1,0:T(8,128)(2,1)} fusion(bf16[1,768,2048]{2,1,0:T(8,128)(2,1)} %all-gather.14.cloned.1.call-done, f32[1024,768]{1,0:T(8,128)S(1)} %fusion.1, bf16[1024,2048]{1,0:T(8,128)(2,1)} %bitcast.4, bf16[1,2048,768]{2,1,0:T(8,128)(2,1)} %all-gather.10.cloned.1.call-done), kind=kOutput, calls=%fused_computation.3 | convolution fusion | flops 6449266688 | bytes 17825792 | tf_op jit(solution)/shard_map/dot_general | solution.py:34
  160.9 4.9 %all-to-all-start.1 = ((bf16[8,128,2048]{2,1,0:T(8,128)(2,1)}), bf16[8,128,2048]{2,1,0:T(8,128)(2,1)}, u32[]{:S(2)}, u32[]{:S(2)}) async-start(bf16[8,128,2048]{2,1,0:T(8,128)(2,1)} %bitcast.29), calls=%async_computation.1 | async-start | bytes 8388608 | tf_op jit(solution)/shard_map/all_to_all | solution.py:39
  165.9 93.9 %all-to-all-done.1 = bf16[8,128,2048]{2,1,0:T(8,128)(2,1)} async-done(((bf16[8,128,2048]{2,1,0:T(8,128)(2,1)}), bf16[8,128,2048]{2,1,0:T(8,128)(2,1)}, u32[]{:S(2)}, u32[]{:S(2)}) %all-to-all-start.1) | async-done | bytes 4194336 | tf_op jit(solution)/shard_map/all_to_all | solution.py:39
  259.8 9.1 %gather_fusion = bf16[768,2048]{1,0:T(8,128)(2,1)S(1)} fusion(bf16[1024,2048]{1,0:T(8,128)(2,1)} %bitcast.9, s32[1024]{0:T(1024)S(1)} %pad_clamp_fusion), kind=kCustom, calls=%fused_computation | custom fusion | bytes 6294528 | tf_op jit(solution)/shard_map/gather | solution.py:40
  268.8 3.7 %reshape.74 = f32[128,6,2048]{2,1,0:T(8,128)} reshape(bf16[768,2048]{1,0:T(8,128)(2,1)S(1)} %gather_fusion) | data formatting | bytes 9437184 | tf_op jit(solution)/shard_map/convert_element_type | solution.py:40
  272.6 6.6 %multiply_reduce_fusion = f32[128,2048]{1,0:T(8,128)S(1)} fusion(f32[128,6,2048]{2,1,0:T(8,128)} %reshape.74, f32[128,6]{1,0:T(8,128)S(1)} %copy.18), kind=kLoop, calls=%fused_computation.2 | loop fusion | flops 2883584 | bytes 7343104 | tf_op jit(solution)/shard_map/reduce_sum | solution.py:41
  279.2 0.9 multiply_reduce_fusion.1
  280.1 4.6 %convolution_convert_fusion.1 = bf16[128,1536]{1,0:T(8,128)(2,1)} fusion(bf16[2048,1536]{1,0:T(8,128)(2,1)} %all-gather.8.cloned.1.call-done, f32[2048]{0:T(1024)S(1)} %copy-done.1, f32[128]{0:T(128)S(1)} %add_rsqrt_fusion, f32[128,2048]{1,0:T(8,128)S(1)} %multiply_reduce_fusion, bf16[128,2048]{1,0:T(8,128)(2,1)S(1)} %copy-done), kind=kOutput, calls=%fused_computation.10 | convolution fusion | flops 806813696 | bytes 8266240 | tf_op jit(solution)/shard_map/dot_general | solution.py:44
  (25 shorter events, 1.2 us)
Async XLA Ops:
  7.2 49.4 %all-gather.12.cloned.1.call-start = ((), (), s32[]{:S(2)}) async-start(), calls=%async_computation.4 | async-start | bytes 3932160 | tf_op jit(solution)/shard_map/all_gather | solution.py:30
  7.9 129.9 %all-gather.10.cloned.1.call-start = ((), (), s32[]{:S(2)}) async-start(), calls=%async_computation.3 | async-start | bytes 3932160 | tf_op jit(solution)/shard_map/all_gather | solution.py:25
  31.0 100.5 %all-to-all-start = ((bf16[8,128,2048]{2,1,0:T(8,128)(2,1)}), bf16[8,128,2048]{2,1,0:T(8,128)(2,1)}, u32[]{:S(2)}, u32[]{:S(2)}) async-start(bf16[8,128,2048]{2,1,0:T(8,128)(2,1)} %bitcast.28), calls=%async_computation | async-start | bytes 8388608 | tf_op jit(solution)/shard_map/all_to_all | solution.py:22
  37.4 110.8 %all-gather.14.cloned.1.call-start = ((), (), s32[]{:S(2)}) async-start(), calls=%async_computation.5 | async-start | bytes 3932160 | tf_op jit(solution)/shard_map/all_gather | solution.py:36
  38.1 242.0 %all-gather.8.cloned.1.call-start = ((), (), s32[]{:S(2)}) async-start(), calls=%async_computation.2 | async-start | bytes 7864320 | tf_op jit(solution)/shard_map/all_gather | solution.py:46
  160.9 4.9 %copy-start.2 = (f32[128,6]{0,1:T(8,128)S(1)}, f32[128,6]{0,1:T(8,128)}, u32[]{:S(2)}) copy-start(f32[128,6]{0,1:T(8,128)} %param.10) | copy-start | bytes 9220
  160.9 98.9 %all-to-all-start.1 = ((bf16[8,128,2048]{2,1,0:T(8,128)(2,1)}), bf16[8,128,2048]{2,1,0:T(8,128)(2,1)}, u32[]{:S(2)}, u32[]{:S(2)}) async-start(bf16[8,128,2048]{2,1,0:T(8,128)(2,1)} %bitcast.29), calls=%async_computation.1 | async-start | bytes 8388608 | tf_op jit(solution)/shard_map/all_to_all | solution.py:39
  272.6 6.6 %copy-start = (bf16[128,2048]{1,0:T(8,128)(2,1)S(1)}, bf16[128,2048]{1,0:T(8,128)(2,1)}, u32[]{:S(2)}) copy-start(bf16[128,2048]{1,0:T(8,128)(2,1)} %param.8) | copy-start | bytes 1572868
  272.6 7.6 %copy-start.1 = (f32[2048]{0:T(1024)S(1)}, f32[2048]{0:T(1024)}, u32[]{:S(2)}) copy-start(f32[2048]{0:T(1024)} %param.14) | copy-start | bytes 24580
Sparse Core Ops, SparseCore 0:
  9.8 46.7 all-gather.11
  58.4 43.9 all-gather.9
  104.3 43.8 all-gather.13
  149.8 70.0 all-gather.7
where the time goes:
time: 292 us; the launch traced here: 291 us
  waiting for transfers between devices  200 us (68%)
  local copies, waits for them, and re-layouts  32.5 us (11%)
  matrix products  23.6 us (8%)
  between operations  13.9 us (5%)
  starting transfers between devices  11.4 us (4%)
  other arithmetic  10.2 us (3%)
    all_to_all x1, waiting for transfers between devices, shards(): lax.all_to_all(answers, 'ep', split_axis=0, concat_axis=0, tiled=True)  93.9 us
    all_to_all x1, waiting for transfers between devices, shards(): lax.all_to_all(outbound, 'ep', split_axis=0, concat_axis=0, tiled=True)  74.9 us
    all_gather x1, waiting for transfers between devices, shards(): lax.all_gather(up_weight[0], 'grp', axis=0, tiled=True)  17.9 us
    dot_general x1, matrix products, shards(): jnp.dot(hidden, lax.all_gather(down_weight[0], 'grp', axis=1, tiled=True)...  12.8 us
    all_gather x1, waiting for transfers between devices, shards(): lax.all_gather(down_weight[0], 'grp', axis=1, tiled=True)  10.4 us
    scatter x1, local copies, waits for them, and re-layouts, shards(): jnp.zeros((ep_count * capacity, width), jnp.bfloat16).at[slot].set(repeated)  9.39 us
    gather x1, local copies, waits for them, and re-layouts, shards(): picked = returned[slot].reshape(tok_rows, choose, width).astype(jnp.float32)  9.06 us
    reduce_sum x1, other arithmetic, shards(): jnp.sum(picked * route_gain[:, :, None], axis=1)  6.59 us
  transfers between devices with their start and end apart: 6, of which 4 were waited for; matrix products, arithmetic and copies ran while one was open for 21% of the time, Pallas kernels for 0%

commit v1 on v0

v1 whole, which is shorter than its diff:
```python
import jax
import jax.numpy as jnp
from jax import lax
from jax.sharding import PartitionSpec as P


def shards(
    tokens, routes, route_gain, gate_weight, up_weight, down_weight, norm_gain, query_weight
):
    ep = lax.axis_index("ep")
    rows = lax.all_gather(tokens, "ep", axis=0, tiled=True)
    named = lax.all_gather(routes, "ep", axis=0, tiled=True)
    gains = lax.all_gather(route_gain, "ep", axis=0, tiled=True)
    scale = jnp.sum(jnp.where(named == ep, gains, 0.0), axis=1, keepdims=True)
    gate = jnp.dot(
        rows,
        lax.all_gather(gate_weight[0], "grp", axis=0, tiled=True),
        preferred_element_type=jnp.float32,
    )
    up = jnp.dot(
        rows,
        lax.all_gather(up_weight[0], "grp", axis=0, tiled=True),
        preferred_element_type=jnp.float32,
    )
    hidden = (jax.nn.silu(gate) * up).astype(jnp.bfloat16)
    answers = jnp.dot(
        hidden,
        lax.all_gather(down_weight[0], "grp", axis=1, tiled=True),
        preferred_element_type=jnp.float32,
    )
    answers = (answers * scale).astype(jnp.bfloat16)
    summed = lax.psum_scatter(answers, "ep", scatter_dimension=0, tiled=True)
    total = tokens.astype(jnp.float32) + summed.astype(jnp.float32)
    square = jnp.mean(total * total, axis=-1, keepdims=True)
    normed = (total * lax.rsqrt(square + 1e-06) * norm_gain).astype(jnp.bfloat16)
    query = jnp.dot(
        normed,
        lax.all_gather(query_weight, "grp", axis=1, tiled=True),
        preferred_element_type=jnp.float32,
    ).astype(jnp.bfloat16)
    return (total.astype(jnp.bfloat16), query)


def solution(mesh):
    placed = (
        P(("grp", "ep"), None),
        P(("grp", "ep"), None),
        P(("grp", "ep"), None),
        P("ep", "grp", None),
        P("ep", "grp", None),
        P("ep", None, "grp"),
        P(),
        P(None, "grp"),
    )
    return jax.shard_map(
        shards,
        mesh=mesh,
        in_specs=placed,
        out_specs=(P(("grp", "ep"), None), P(("grp", "ep"), None)),
        check_vma=False,
    )
```

time: 292 us -> 340 us (1.16)
  waiting for transfers between devices: 200 us -> 270 us
  local copies, waits for them, and re-layouts: 32.5 us -> 0.01 us
  blocking collectives: 0 us -> 29.9 us
  starting transfers between devices: 11.4 us -> 0.23 us
  other arithmetic: 10.2 us -> 2.05 us
    all_to_all x2 -> x0, waiting for transfers between devices: 169 us -> none  [the longest x1 93.9 us: shards(): lax.all_to_all(answers, 'ep', split_axis=0, concat_axis=0, tiled=True)]
    all_gather x1, waiting for transfers between devices: 0.01 us -> 67.9 us  [shards(): lax.all_gather(query_weight, 'grp', axis=1, tiled=True)]
    reduce_scatter x0 -> x1, waiting for transfers between devices: none -> 49.6 us  [shards(): summed = lax.psum_scatter(answers, 'ep', scatter_dimension=0, tiled=True)]
    all_gather x0 -> x1, waiting for transfers between devices: none -> 48.8 us  [shards(): rows = lax.all_gather(tokens, 'ep', axis=0, tiled=True)]
    all_gather x1, waiting for transfers between devices: 0.02 us -> 38.4 us  [shards(): lax.all_gather(gate_weight[0], 'grp', axis=0, tiled=True)]
    all_gather x1, waiting for transfers between devices: 10.4 us -> 45.5 us  [shards(): lax.all_gather(down_weight[0], 'grp', axis=1, tiled=True)]
    all_gather x0 -> x2, blocking collectives: none -> 29.9 us  [the longest x1 15.8 us: shards(): named = lax.all_gather(routes, 'ep', axis=0, tiled=True)]
    all_to_all x2 -> x0, starting transfers between devices: 11.2 us -> none  [the longest x1 6.39 us: shards(): lax.all_to_all(outbound, 'ep', split_axis=0, concat_axis=0, tiled=True)]
  transfers between devices with their start and end apart: 6 -> 6, of which waited for: 4 -> 6; matrix products, arithmetic and copies ran while one was open for 21% -> 2% of each run, Pallas kernels for 0% -> 0%
where the time goes in v1:
time: 340 us
  waiting for transfers between devices  270 us (79%)
  blocking collectives  29.9 us (9%)
  matrix products  23.7 us (7%)
  between operations  14.1 us (4%)
    all_gather x1, waiting for transfers between devices, shards(): lax.all_gather(query_weight, 'grp', axis=1, tiled=True)  67.9 us
    reduce_scatter x1, waiting for transfers between devices, shards(): summed = lax.psum_scatter(answers, 'ep', scatter_dimension=0, tiled=True)  49.6 us
    all_gather x1, waiting for transfers between devices, shards(): rows = lax.all_gather(tokens, 'ep', axis=0, tiled=True)  48.8 us
    all_gather x1, waiting for transfers between devices, shards(): lax.all_gather(down_weight[0], 'grp', axis=1, tiled=True)  45.5 us
    all_gather x1, waiting for transfers between devices, shards(): lax.all_gather(gate_weight[0], 'grp', axis=0, tiled=True)  38.4 us
    all_gather x1, waiting for transfers between devices, shards(): lax.all_gather(up_weight[0], 'grp', axis=0, tiled=True)  16.6 us
    all_gather x1, blocking collectives, shards(): named = lax.all_gather(routes, 'ep', axis=0, tiled=True)  15.8 us
    all_gather x1, blocking collectives, shards(): gains = lax.all_gather(route_gain, 'ep', axis=0, tiled=True)  14.1 us
  transfers between devices with their start and end apart: 6, of which 6 were waited for; matrix products, arithmetic and copies ran while one was open for 2% of the time, Pallas kernels for 0%

profile of v1, /device:TPU:0, one launch (start us, length us, event | category | flops | bytes accessed | tf_op | source)
XLA Modules:
  0.0 340.0 jit_solution(9775812223790886335)
XLA Ops:
  7.2 0.0 all-gather.15.cloned.1.call-start
  7.2 0.7 all-gather.15.cloned.1.call-update
  7.9 0.0 all-gather.9.cloned.1.call-start
  7.9 0.7 all-gather.9.cloned.1.call-update
  8.6 0.0 all-gather.13.cloned.1.call-start
  8.7 0.7 all-gather.13.cloned.1.call-update
  9.4 0.0 all-gather.17.cloned.1.call-start
  9.4 0.5 all-gather.17.cloned.1.call-update
  10.0 0.0 reduce-scatter.2.cloned.1.call-start
  10.0 15.8 %all_gather.25 = s32[1024,6]{0,1:T(8,128)S(1)} all-gather(s32[128,6]{0,1:T(8,128)} %param.9), channel_id=1, replica_groups=mesh['grp'=4,'ep'=8] {'ep'}, dimensions={0}, use_global_device_ids=true | all-gather | bytes 27648 | tf_op jit(solution)/shard_map/all_gather | solution.py:12
  25.8 14.1 %all_gather.26 = f32[1024,6]{0,1:T(8,128)S(1)} all-gather(f32[128,6]{0,1:T(8,128)} %param.10), channel_id=1, replica_groups=mesh['grp'=4,'ep'=8] {'ep'}, dimensions={0}, use_global_device_ids=true | all-gather | bytes 27648 | tf_op jit(solution)/shard_map/all_gather | solution.py:13
  40.0 16.6 %all-gather.15.cloned.1.call-done = bf16[1,2048,768]{2,1,0:T(8,128)(2,1)} async-done(((bf16[1,512,768]{2,1,0:T(8,128)(2,1)}), bf16[1,2048,768]{2,1,0:T(8,128)(2,1)}) %all-gather.15.cloned.1.call-update) | async-done | bytes 3145744 | tf_op jit(solution)/shard_map/all_gather | solution.py:22
  56.5 48.8 %all-gather.9.cloned.1.call-done = bf16[1024,2048]{1,0:T(8,128)(2,1)} async-done(((bf16[128,2048]{1,0:T(8,128)(2,1)}), bf16[1024,2048]{1,0:T(8,128)(2,1)}) %all-gather.9.cloned.1.call-update) | async-done | bytes 4194320 | tf_op jit(solution)/shard_map/all_gather | solution.py:11
  105.3 6.1 %fusion.1 = f32[1024,768]{1,0:T(8,128)S(1)} fusion(bf16[1024,2048]{1,0:T(8,128)(2,1)} %all-gather.9.cloned.1.call-done, bf16[1,2048,768]{2,1,0:T(8,128)(2,1)} %all-gather.15.cloned.1.call-done), kind=kOutput, calls=%fused_computation.2 | convolution fusion | flops 3221225472 | bytes 10485760 | tf_op jit(solution)/shard_map/dot_general | solution.py:20
  111.5 38.4 %all-gather.13.cloned.1.call-done = bf16[1,2048,768]{2,1,0:T(8,128)(2,1)} async-done(((bf16[1,512,768]{2,1,0:T(8,128)(2,1)}), bf16[1,2048,768]{2,1,0:T(8,128)(2,1)}) %all-gather.13.cloned.1.call-update) | async-done | bytes 3145744 | tf_op jit(solution)/shard_map/all_gather | solution.py:17
  149.9 45.5 %all-gather.17.cloned.1.call-done = bf16[1,768,2048]{2,1,0:T(8,128)(2,1)} async-done(((bf16[1,768,512]{2,1,0:T(8,128)(2,1)}), bf16[1,768,2048]{2,1,0:T(8,128)(2,1)}) %all-gather.17.cloned.1.call-update) | async-done | bytes 3145744 | tf_op jit(solution)/shard_map/all_gather | solution.py:28
  195.5 12.8 %multiply_convert_fusion = bf16[1024,2048]{1,0:T(8,128)(2,1)} fusion(f32[1024]{0:T(1024)S(1)} %select_reduce_fusion, bf16[1,768,2048]{2,1,0:T(8,128)(2,1)} %all-gather.17.cloned.1.call-done, f32[1024,768]{1,0:T(8,128)S(1)} %fusion.1, bf16[1024,2048]{1,0:T(8,128)(2,1)} %all-gather.9.cloned.1.call-done, bf16[1,2048,768]{2,1,0:T(8,128)(2,1)} %all-gather.13.cloned.1.call-done), kind=kOutput, calls=%fused_computation | convolution fusion | flops 6451363840 | bytes 17829888 | tf_op jit(solution)/shard_map/dot_general | solution.py:26
  208.3 0.0 reduce-scatter.2.cloned.1.call-update
  208.3 0.0 all-gather.11.cloned.1.call-start
  208.3 0.5 all-gather.11.cloned.1.call-update
  208.9 49.6 %reduce-scatter.2.cloned.1.call-done = bf16[128,2048]{1,0:T(8,128)(2,1)} async-done(((bf16[1024,2048]{1,0:T(8,128)(2,1)}), bf16[128,2048]{1,0:T(8,128)(2,1)}) %reduce-scatter.2.cloned.1.call-update) | async-done | bytes 524304 | tf_op jit(solution)/shard_map/reduce_scatter | solution.py:32
  258.5 2.0 multiply_reduce_fusion
  260.5 67.9 %all-gather.11.cloned.1.call-done = bf16[2048,1536]{1,0:T(8,128)(2,1)} async-done(((bf16[2048,384]{1,0:T(8,128)(2,1)}), bf16[2048,1536]{1,0:T(8,128)(2,1)}) %all-gather.11.cloned.1.call-update) | async-done | bytes 6291472 | tf_op jit(solution)/shard_map/all_gather | solution.py:38
  328.4 4.8 %convolution_convert_fusion = bf16[128,1536]{1,0:T(8,128)(2,1)} fusion(bf16[2048,1536]{1,0:T(8,128)(2,1)} %all-gather.11.cloned.1.call-done, bf16[128,2048]{1,0:T(8,128)(2,1)} %reduce-scatter.2.cloned.1.call-done, bf16[128,2048]{1,0:T(8,128)(2,1)S(1)} %copy-done, f32[2048]{0:T(1024)S(1)} %copy-done.1, f32[128]{0:T(128)S(1)} %add_rsqrt_fusion), kind=kOutput, calls=%fused_computation.7 | convolution fusion | flops 807075840 | bytes 7741952 | tf_op jit(solution)/shard_map/dot_general | solution.py:36
  (6 shorter events, 0.0 us)
Async XLA Ops:
  7.2 49.4 %all-gather.15.cloned.1.call-start = ((), (), s32[]{:S(2)}) async-start(), calls=%async_computation.5 | async-start | bytes 3932160 | tf_op jit(solution)/shard_map/all_gather | solution.py:22
  7.9 97.4 %all-gather.9.cloned.1.call-start = ((), (), s32[]{:S(2)}) async-start(), calls=%async_computation.1 | async-start | bytes 4718592 | tf_op jit(solution)/shard_map/all_gather | solution.py:11
  8.6 141.3 %all-gather.13.cloned.1.call-start = ((), (), s32[]{:S(2)}) async-start(), calls=%async_computation.4 | async-start | bytes 3932160 | tf_op jit(solution)/shard_map/all_gather | solution.py:17
  9.4 186.1 %all-gather.17.cloned.1.call-start = ((), (), s32[]{:S(2)}) async-start(), calls=%async_computation.6 | async-start | bytes 3932160 | tf_op jit(solution)/shard_map/all_gather | solution.py:28
  10.0 248.5 %reduce-scatter.2.cloned.1.call-start = ((), (), s32[]{:S(2)}) async-start(), calls=%async_computation.2 | async-start | bytes 4718592 | tf_op jit(solution)/shard_map/reduce_scatter | solution.py:32
  208.3 50.2 %copy-start = (bf16[128,2048]{1,0:T(8,128)(2,1)S(1)}, bf16[128,2048]{1,0:T(8,128)(2,1)}, u32[]{:S(2)}) copy-start(bf16[128,2048]{1,0:T(8,128)(2,1)} %param.8) | copy-start | bytes 1572868
  208.3 120.1 %copy-start.1 = (f32[2048]{0:T(1024)S(1)}, f32[2048]{0:T(1024)}, u32[]{:S(2)}) copy-start(f32[2048]{0:T(1024)} %param.14) | copy-start | bytes 24580
  208.3 120.1 %all-gather.11.cloned.1.call-start = ((), (), s32[]{:S(2)}) async-start(), calls=%async_computation.3 | async-start | bytes 7864320 | tf_op jit(solution)/shard_map/all_gather | solution.py:38
Sparse Core Ops, SparseCore 0:
  9.8 46.6 all-gather.14
  58.1 47.1 all-gather.8
  107.2 42.6 all-gather.12
  151.6 43.8 all-gather.16
  208.4 50.0 reduce-scatter.1
  260.1 68.1 all-gather.10

commit v2 on v0

--- a/solution.py
+++ b/solution.py
@@ -1,10 +1,442 @@
 import jax
 import jax.numpy as jnp
 from jax import lax
+from jax.experimental import pallas as pl
+from jax.experimental.pallas import tpu as pltpu
 from jax.sharding import PartitionSpec as P
 
-
-def shards(
+MESH = pl.DeviceIdType.MESH
+NZ = 4
+
+
+def kernel(
+    tok, gtab, gw, uw, dw, ng, qw, mixed, query,
+    rows, gains, scale, gin, uin, din, qin, acc_g, acc_u, hid,
+    sout, sin, part, rin, lin, rout, total, normed,
+    gain_s, gain_r, tok_r, tok_sr, tok_sl, tok_ss, w_s, w_r, q_s, q_r,
+    sib_s, sib_r, right_s, right_r, left_s, left_r,
+):
+    g = lax.axis_index("grp")
+    ep = lax.axis_index("ep")
+    z = ep // 2
+    c = ep % 2
+    gx = g + 1 - 2 * (g % 2)
+    gy = (g + 2) % 4
+    gd = 3 - g
+    x_dev, y_dev = (gx, ep), (gy, ep)
+    sib = (g, ep + 1 - 2 * c)
+    nxt, prv = (g, ep + 2), (g, ep - 2)
+    n_tok, width = tok.shape
+    depth = gw.shape[0]
+    cols = dw.shape[1]
+    qcols = qw.shape[1]
+    has_next, has_prev = z < NZ - 1, z > 0
+
+    def remote(src, dst, s, r, dev):
+        return pltpu.make_async_remote_copy(
+            src_ref=src, dst_ref=dst, send_sem=s, recv_sem=r, device_id=dev, device_id_type=MESH
+        )
+
+    barrier = pltpu.get_barrier_semaphore()
+    for k in range(1, 2 * NZ):
+        pl.semaphore_signal(barrier, inc=1, device_id=(g, (ep + k) % (2 * NZ)), device_id_type=MESH)
+    for dev in (x_dev, y_dev):
+        pl.semaphore_signal(barrier, inc=1, device_id=dev, device_id_type=MESH)
+    pl.semaphore_wait(barrier, 2 * NZ + 1)
+
+    def block(zz, cc):
+        return rows.at[pl.ds(pl.multiple_of((cc * NZ + zz) * n_tok, n_tok), n_tok)]
+
+    def tok_copy(src, zz, send, dev):
+        return remote(src, block(zz, c), send.at[zz], tok_r.at[c * NZ + zz], dev)
+
+    def tok_wait(zz, cc):
+        ref = block(zz, cc)
+        remote(ref, ref, tok_ss.at[0], tok_r.at[cc * NZ + zz], sib).wait_recv()
+
+    @pl.when(has_next)
+    def _():
+        tok_copy(tok, z, tok_sr, nxt).start()
+
+    @pl.when(has_prev)
+    def _():
+        tok_copy(tok, z, tok_sl, prv).start()
+
+    tok_copy(tok, z, tok_ss, sib).start()
+
+    shards_of = ((gw, gin), (uw, uin), (dw, din))
+
+    def own_x(i):
+        src, dst = shards_of[i]
+        return remote(src, dst.at[0], w_s.at[i, 0], w_r.at[i, 0], x_dev)
+
+    def own_y(i):
+        src, dst = shards_of[i]
+        return remote(src, dst.at[1], w_s.at[i, 1], w_r.at[i, 1], y_dev)
+
+    def relay_y(i):
+        dst = shards_of[i][1]
+        half = dst.shape[1] // 2
+        return remote(
+            dst.at[0, pl.ds(0, half)], dst.at[2, pl.ds(0, half)], w_s.at[i, 2], w_r.at[i, 2], y_dev
+        )
+
+    def relay_x(i):
+        dst = shards_of[i][1]
+        half = dst.shape[1] // 2
+        return remote(
+            dst.at[1, pl.ds(half, half)], dst.at[2, pl.ds(half, half)],
+            w_s.at[i, 3], w_r.at[i, 3], x_dev,
+        )
+
+    own_x(0).start()
+    own_y(0).start()
+    own_x(1).start()
+    own_y(1).start()
+
+    def gain_copy(k):
+        return remote(
+            gtab, gains.at[c * NZ + z], gain_s.at[k], gain_r.at[c * NZ + z],
+            (g, (ep + k) % (2 * NZ)),
+        )
+
+    for k in range(1, 2 * NZ):
+        gain_copy(k).start()
+
+    rows[pl.ds(pl.multiple_of((c * NZ + z) * n_tok, n_tok), n_tok), :] = tok[...]
+    gains[c * NZ + z] = gtab[...]
+
+    def hop(h):
+        left, right = z - 1 - h, z + 1 + h
+
+        @pl.when(left >= 0)
+        def _():
+            tok_wait(left, c)
+
+            @pl.when(has_next)
+            def _():
+                tok_copy(block(left, c), left, tok_sr, nxt).start()
+
+            tok_copy(block(left, c), left, tok_ss, sib).start()
+
+        @pl.when(right <= NZ - 1)
+        def _():
+            tok_wait(right, c)
+
+            @pl.when(has_prev)
+            def _():
+                tok_copy(block(right, c), right, tok_sl, prv).start()
+
+            tok_copy(block(right, c), right, tok_ss, sib).start()
+
+    def pass_on(i):
+        own_x(i).wait_recv()
+        relay_y(i).start()
+        own_y(i).wait_recv()
+        relay_x(i).start()
+
+    hop(0)
+    hop(1)
+    pass_on(0)
+    hop(2)
+    pass_on(1)
+
+    for k in range(1, 2 * NZ):
+        peer = (ep + k) % (2 * NZ)
+        at = (peer % 2) * NZ + peer // 2
+        remote(gtab, gains.at[at], gain_s.at[0], gain_r.at[at], sib).wait_recv()
+    for b in range(2 * NZ):
+        table = gains[b]
+        chosen = lax.broadcasted_iota(jnp.int32, table.shape, 0) == ep
+        line = jnp.sum(jnp.where(chosen, table, 0.0), axis=0, keepdims=True)
+        scale[b * n_tok : (b + 1) * n_tok, :] = jnp.broadcast_to(line, (n_tok, n_tok)).T
+    for zz in range(NZ):
+        tok_wait(zz, 1 - c)
+
+    tile = 2 * n_tok
+    tiles = rows.shape[0] // tile
+
+    def partial(acc, w, owner, first):
+        at = pl.ds(pl.multiple_of(owner * depth, depth), depth)
+
+        def body(i, carry):
+            r = pl.ds(pl.multiple_of(i * tile, tile), tile)
+            p = jnp.dot(rows[r, at], w[...], preferred_element_type=jnp.float32)
+            acc[r, :] = p if first else acc[r, :] + p
+            return carry
+
+        lax.fori_loop(0, tiles, body, 0)
+
+    partial(acc_g, gw, g, True)
+    partial(acc_u, uw, g, True)
+    partial(acc_g, gin.at[0], gx, False)
+    partial(acc_g, gin.at[1], gy, False)
+    partial(acc_u, uin.at[0], gx, False)
+    partial(acc_u, uin.at[1], gy, False)
+    relay_y(0).wait_recv()
+    relay_x(0).wait_recv()
+    own_x(2).start()
+    own_y(2).start()
+    partial(acc_g, gin.at[2], gd, False)
+    relay_y(1).wait_recv()
+    relay_x(1).wait_recv()
+    partial(acc_u, uin.at[2], gd, False)
+
+    def act(i, carry):
+        r = pl.ds(pl.multiple_of(i * n_tok, n_tok), n_tok)
+        gate = acc_g[r, :]
+        hid[r, :] = (gate / (1.0 + jnp.exp(-gate)) * acc_u[r, :]).astype(hid.dtype)
+        return carry
+
+    lax.fori_loop(0, rows.shape[0] // n_tok, act, 0)
+
+    def sib_copy(q):
+        return remote(sout.at[q], sin.at[q], sib_s.at[q], sib_r.at[q], sib)
+
+    def answers(q, w):
+        per = tile // n_tok
+
+        def weighted(cc, i):
+            at = pl.multiple_of(cc * NZ * n_tok + i * tile, tile)
+            p = jnp.dot(hid[pl.ds(at, tile), :], w[...], preferred_element_type=jnp.float32)
+            s = scale[pl.ds(at, tile), :]
+            p = p * jnp.concatenate([s] * (cols // n_tok), axis=1)
+            return p.reshape(per, n_tok, cols)
+
+        def away(i, carry):
+            sout[q, pl.ds(i * per, per)] = weighted(1 - c, i).astype(sout.dtype)
+            return carry
+
+        def here(i, carry):
+            part[q, pl.ds(i * per, per)] = weighted(c, i)
+            return carry
+
+        lax.fori_loop(0, NZ // per, away, 0)
+        sib_copy(q).start()
+        lax.fori_loop(0, NZ // per, here, 0)
+        sib_copy(q).wait_recv()
+
+    def right_copy(q, d):
+        return remote(rout.at[q, d], rin.at[q, d], right_s.at[q, d], right_r.at[q, d], nxt)
+
+    def left_copy(q, d):
+        return remote(rout.at[q, d], lin.at[q, d], left_s.at[q, d], left_r.at[q, d], prv)
+
+    def ends(q):
+        @pl.when(z == 0)
+        def _():
+            for d in range(NZ - 1, 0, -1):
+                rout[q, d] = (part[q, d] + sin[q, d].astype(jnp.float32)).astype(rout.dtype)
+                right_copy(q, d).start()
+
+        @pl.when(z == NZ - 1)
+        def _():
+            for d in range(NZ - 1):
+                rout[q, d] = (part[q, d] + sin[q, d].astype(jnp.float32)).astype(rout.dtype)
+                left_copy(q, d).start()
+
+    def chain(q, owner):
+        for k in range(NZ - 1):
+            d = NZ - 1 - k
+
+            @pl.when((z > 0) & (z < d))
+            def _():
+                right_copy(q, d).wait_recv()
+                rout[q, d] = (
+                    part[q, d] + sin[q, d].astype(jnp.float32) + rin[q, d].astype(jnp.float32)
+                ).astype(rout.dtype)
+                right_copy(q, d).start()
+
+            @pl.when((z < NZ - 1) & (z > k))
+            def _():
+                left_copy(q, k).wait_recv()
+                rout[q, k] = (
+                    part[q, k] + sin[q, k].astype(jnp.float32) + lin[q, k].astype(jnp.float32)
+                ).astype(rout.dtype)
+                left_copy(q, k).start()
+
+        at = pl.ds(pl.multiple_of(owner * cols, cols), cols)
+        total[:, at] = tok[:, at].astype(jnp.float32) + part[q, z] + sin[q, z].astype(jnp.float32)
+
+        @pl.when(has_prev)
+        def _():
+            right_copy(q, z).wait_recv()
+            total[:, at] = total[:, at] + rin[q, z].astype(jnp.float32)
+
+        @pl.when(has_next)
+        def _():
+            left_copy(q, z).wait_recv()
+            total[:, at] = total[:, at] + lin[q, z].astype(jnp.float32)
+
+    q_half = qw.shape[0] // 2
+    q_quarter = q_half // 2
+    half_at = pl.ds(pl.multiple_of(c * q_half, q_half), q_half)
+    first_at = pl.ds(pl.multiple_of(c * q_half, q_quarter), q_quarter)
+    second_at = pl.ds(pl.multiple_of(c * q_half + q_quarter, q_quarter), q_quarter)
+
+    def q_copy(k):
+        if k == 0:
+            return remote(qw.at[half_at], qin.at[0, half_at], q_s.at[0], q_r.at[0], x_dev)
+        if k == 1:
+            return remote(qw.at[half_at], qin.at[1, half_at], q_s.at[1], q_r.at[1], y_dev)
+        if k == 2:
+            return remote(qin.at[0, first_at], qin.at[2, first_at], q_s.at[2], q_r.at[2], y_dev)
+        if k == 3:
+            return remote(qin.at[1, second_at], qin.at[2, second_at], q_s.at[3], q_r.at[3], x_dev)
+        slot, at = ((0, half_at), (1, half_at), (2, first_at), (2, second_at))[k - 4]
+        return remote(qin.at[slot, at], qin.at[slot, at], q_s.at[k], q_r.at[k], sib)
+
+    other_half = pl.ds(pl.multiple_of((1 - c) * q_half, q_half), q_half)
+    other_first = pl.ds(pl.multiple_of((1 - c) * q_half, q_quarter), q_quarter)
+    other_second = pl.ds(pl.multiple_of((1 - c) * q_half + q_quarter, q_quarter), q_quarter)
+
+    def q_wait_sib(k):
+        slot, at = ((0, other_half), (1, other_half), (2, other_first), (2, other_second))[k - 4]
+        remote(qin.at[slot, at], qin.at[slot, at], q_s.at[k], q_r.at[k], sib).wait_recv()
+
+    answers(0, dw)
+    ends(0)
+    chain(0, g)
+    pass_on(2)
+    answers(1, din.at[0])
+    ends(1)
+    answers(2, din.at[1])
+    ends(2)
+    relay_y(2).wait_recv()
+    relay_x(2).wait_recv()
+    q_copy(0).start()
+    q_copy(1).start()
+    chain(1, gx)
+    answers(3, din.at[2])
+    ends(3)
+    chain(2, gy)
+    q_copy(0).wait_recv()
+    q_copy(2).start()
+    q_copy(4).start()
+    q_copy(1).wait_recv()
+    q_copy(3).start()
+    q_copy(5).start()
+    chain(3, gd)
+
+    value = total[...]
+    mixed[...] = value.astype(mixed.dtype)
+    square = jnp.sum(value * value, axis=-1, keepdims=True) * (1.0 / width)
+    normed[...] = (value * lax.rsqrt(square + 1e-06) * ng[...]).astype(normed.dtype)
+
+    def project(w, owner):
+        at = pl.ds(pl.multiple_of(owner * qcols, qcols), qcols)
+        query[:, at] = jnp.dot(
+            normed[...], w[...], preferred_element_type=jnp.float32
+        ).astype(query.dtype)
+
+    project(qw, g)
+    q_wait_sib(4)
+    project(qin.at[0], gx)
+    q_wait_sib(5)
+    project(qin.at[1], gy)
+    q_copy(2).wait_recv()
+    q_copy(6).start()
+    q_copy(3).wait_recv()
+    q_copy(7).start()
+    q_wait_sib(6)
+    q_wait_sib(7)
+    project(qin.at[2], gd)
+
+    for k in range(1, 2 * NZ):
+        gain_copy(k).wait_send()
+    for zz in range(NZ):
+        @pl.when(has_next & (zz <= z))
+        def _():
+            tok_copy(tok, zz, tok_sr, nxt).wait_send()
+
+        @pl.when(has_prev & (zz >= z))
+        def _():
+            tok_copy(tok, zz, tok_sl, prv).wait_send()
+
+        tok_copy(tok, zz, tok_ss, sib).wait_send()
+    for i in range(3):
+        for copy in (own_x, own_y, relay_x, relay_y):
+            copy(i).wait_send()
+    for k in range(8):
+        q_copy(k).wait_send()
+    for q in range(4):
+        sib_copy(q).wait_send()
+        for d in range(NZ):
+            if d > 0:
+                @pl.when(z < d)
+                def _():
+                    right_copy(q, d).wait_send()
+            if d < NZ - 1:
+                @pl.when(z > d)
+                def _():
+                    left_copy(q, d).wait_send()
+
+
+def fused(tokens, routes, route_gain, gate_weight, up_weight, down_weight, norm_gain, query_weight):
+    n_tok, width = tokens.shape
+    hidden = gate_weight.shape[2]
+    depth, cols, qcols = gate_weight.shape[1], down_weight.shape[2], query_weight.shape[1]
+    experts = jnp.arange(2 * NZ, dtype=jnp.int32)
+    named = routes[None, :, :] == experts[:, None, None]
+    gtab = jnp.sum(jnp.where(named, route_gain[None, :, :], 0.0), axis=2)
+    n_rows = 2 * NZ * n_tok
+    vmem = pl.BlockSpec(memory_space=pltpu.VMEM)
+    b16, f32 = jnp.bfloat16, jnp.float32
+    dma = pltpu.SemaphoreType.DMA
+    return pl.pallas_call(
+        kernel,
+        out_shape=(
+            jax.ShapeDtypeStruct((n_tok, width), b16),
+            jax.ShapeDtypeStruct((n_tok, 4 * qcols), b16),
+        ),
+        in_specs=[vmem] * 7,
+        out_specs=(vmem, vmem),
+        scratch_shapes=[
+            pltpu.VMEM((n_rows, width), b16),
+            pltpu.VMEM((2 * NZ, 2 * NZ, n_tok), f32),
+            pltpu.VMEM((n_rows, n_tok), f32),
+            pltpu.VMEM((3, depth, hidden), b16),
+            pltpu.VMEM((3, depth, hidden), b16),
+            pltpu.VMEM((3, hidden, cols), b16),
+            pltpu.VMEM((3, width, qcols), b16),
+            pltpu.VMEM((n_rows, hidden), f32),
+            pltpu.VMEM((n_rows, hidden), f32),
+            pltpu.VMEM((n_rows, hidden), b16),
+            pltpu.VMEM((4, NZ, n_tok, cols), b16),
+            pltpu.VMEM((4, NZ, n_tok, cols), b16),
+            pltpu.VMEM((4, NZ, n_tok, cols), f32),
+            pltpu.VMEM((4, NZ, n_tok, cols), b16),
+            pltpu.VMEM((4, NZ, n_tok, cols), b16),
+            pltpu.VMEM((4, NZ, n_tok, cols), b16),
+            pltpu.VMEM((n_tok, width), f32),
+            pltpu.VMEM((n_tok, width), b16),
+            dma((2 * NZ,)),
+            dma((2 * NZ,)),
+            dma((2 * NZ,)),
+            dma((NZ,)),
+            dma((NZ,)),
+            dma((NZ,)),
+            dma((3, 4)),
+            dma((3, 4)),
+            dma((8,)),
+            dma((8,)),
+            dma((4,)),
+            dma((4,)),
+            dma((4, NZ)),
+            dma((4, NZ)),
+            dma((4, NZ)),
+            dma((4, NZ)),
+        ],
+        compiler_params=pltpu.CompilerParams(
+            collective_id=0, has_side_effects=True, vmem_limit_bytes=60 * 1024 * 1024
+        ),
+    )(
+        tokens, gtab, gate_weight[0], up_weight[0], down_weight[0],
+        norm_gain.reshape(1, width), query_weight,
+    )
+
+
+def general(
     tokens, routes, route_gain, gate_weight, up_weight, down_weight, norm_gain, query_weight
 ):
     ep_count = lax.axis_size("ep")
@@ -60,8 +492,9 @@
         P(),
         P(None, "grp"),
     )
+    small = mesh.shape["grp"] == 4 and mesh.shape["ep"] == 2 * NZ
     return jax.shard_map(
-        shards,
+        fused if small else general,
         mesh=mesh,
         in_specs=placed,
         out_specs=(P(("grp", "ep"), None), P(("grp", "ep"), None)),

time: 292 us -> 144 us (0.49)
  waiting for transfers between devices: 200 us -> 0 us
  Pallas kernels: 0 us -> 138 us
  local copies, waits for them, and re-layouts: 32.5 us -> 3.65 us
  matrix products: 23.6 us -> 0 us
  between operations: 13.9 us -> 0.64 us
  starting transfers between devices: 11.4 us -> 0 us
  other arithmetic: 10.2 us -> 1.31 us
    all_to_all x2 -> x0, waiting for transfers between devices: 169 us -> none  [the longest x1 93.9 us: shards(): lax.all_to_all(answers, 'ep', split_axis=0, concat_axis=0, tiled=True)]
    pallas_call x0 -> x1, Pallas kernels: none -> 138 us  [fused(): pl.pallas_call(kernel, out_shape=(jax.ShapeDtypeStruct((n_tok, width), b1...]
    all_gather x4 -> x0, waiting for transfers between devices: 28.3 us -> none  [the longest x1 17.9 us: shards(): lax.all_gather(up_weight[0], 'grp', axis=0, tiled=True)]
    dot_general x3 -> x0, matrix products: 23.6 us -> none  [the longest x1 12.8 us: shards(): jnp.dot(hidden, lax.all_gather(down_weight[0], 'grp', axis=1, tiled=True)...]
    all_to_all x2 -> x0, starting transfers between devices: 11.2 us -> none  [the longest x1 6.39 us: shards(): lax.all_to_all(outbound, 'ep', split_axis=0, concat_axis=0, tiled=True)]
    scatter x1 -> x0, local copies, waits for them, and re-layouts: 9.39 us -> none  [shards(): jnp.zeros((ep_count * capacity, width), jnp.bfloat16).at[slot].set(repeated)]
    gather x1 -> x0, local copies, waits for them, and re-layouts: 9.06 us -> none  [shards(): picked = returned[slot].reshape(tok_rows, choose, width).astype(jnp.float32)]
    reduce_sum x3 -> x1, other arithmetic: 7.62 us -> 1.31 us  [fused(): gtab = jnp.sum(jnp.where(named, route_gain[None, :, :], 0.0), axis=2)]
  transfers between devices with their start and end apart: 6 -> 0, of which waited for: 4 -> 0; matrix products, arithmetic and copies ran while one was open for 21% -> 0% of each run, Pallas kernels for 0% -> 0%
where the time goes in v2:
time: 144 us
  Pallas kernels  138 us (96%)
  local copies, waits for them, and re-layouts  3.65 us (3%)
    pallas_call x1, Pallas kernels, fused(): pl.pallas_call(kernel, out_shape=(jax.ShapeDtypeStruct((n_tok, width), b1...  138 us
    unnamed x2, local copies, waits for them, and re-layouts  3.65 us

profile of v2, /device:TPU:0, one launch (start us, length us, event | category | flops | bytes accessed | tf_op | source)
XLA Modules:
  0.0 143.7 jit_solution(9931772980996303635)
XLA Ops:
  0.6 1.3 select_reduce_fusion.gtab
  1.9 138.1 %shard_map.95 = (bf16[128,2048]{1,0:T(8,128)(2,1)}, bf16[128,1536]{1,0:T(8,128)(2,1)}) custom-call(bf16[128,2048]{1,0:T(8,128)(2,1)} %tok.1, f32[8,128]{1,0:T(8,128)} %select_reduce_fusion.gtab, bf16[512,768]{1,0:T(8,128)(2,1)} %bitcast.4, bf16[512,768]{1,0:T(8,128)(2,1)} %bitcast.5, bf16[768,512]{1,0:T(8,128)(2,1)} %bitcast.6, f32[1,2048]{1,0:T(1,128)} %bitcast.7, ...), custom_call_target="tpu_custom_call" | custom-call | tf_op jit(solution)/shard_map/pallas_call | solution.py:386
  140.0 1.9 %copy.14 = bf16[128,2048]{1,0:T(8,128)(2,1)} copy(bf16[128,2048]{1,0:T(8,128)(2,1)} %get-tuple-element.4) | data formatting | bytes 1048576
  141.9 1.8 %copy.15 = bf16[128,1536]{1,0:T(8,128)(2,1)} copy(bf16[128,1536]{1,0:T(8,128)(2,1)} %get-tuple-element.5) | data formatting | bytes 786432

commit v3 on v2

--- a/solution.py
+++ b/solution.py
@@ -10,8 +10,8 @@
 
 
 def kernel(
-    tok, gtab, gw, uw, dw, ng, qw, mixed, query,
-    rows, gains, scale, gin, uin, din, qin, acc_g, acc_u, hid,
+    tok, routes, gain, gw, uw, dw, ng, qw, mixed, query,
+    rows, gtab, gains, scale, gin, uin, din, qin, acc_g, acc_u, hid,
     sout, sin, part, rin, lin, rout, total, normed,
     gain_s, gain_r, tok_r, tok_sr, tok_sl, tok_ss, w_s, w_r, q_s, q_r,
     sib_s, sib_r, right_s, right_r, left_s, left_r,
@@ -100,6 +100,11 @@
             (g, (ep + k) % (2 * NZ)),
         )
 
+    expert = lax.broadcasted_iota(jnp.int32, (2 * NZ, n_tok), 0)
+    table = jnp.zeros((2 * NZ, n_tok), jnp.float32)
+    for k in range(routes.shape[0]):
+        table = table + jnp.where(expert == routes[k : k + 1, :], gain[k : k + 1, :], 0.0)
+    gtab[...] = table
     for k in range(1, 2 * NZ):
         gain_copy(k).start()
 
@@ -140,6 +145,8 @@
     pass_on(0)
     hop(2)
     pass_on(1)
+    own_x(2).start()
+    own_y(2).start()
 
     for k in range(1, 2 * NZ):
         peer = (ep + k) % (2 * NZ)
@@ -175,8 +182,6 @@
     partial(acc_u, uin.at[1], gy, False)
     relay_y(0).wait_recv()
     relay_x(0).wait_recv()
-    own_x(2).start()
-    own_y(2).start()
     partial(acc_g, gin.at[2], gd, False)
     relay_y(1).wait_recv()
     relay_x(1).wait_recv()
@@ -296,17 +301,17 @@
 
     answers(0, dw)
     ends(0)
+    pass_on(2)
+    q_copy(0).start()
+    q_copy(1).start()
     chain(0, g)
-    pass_on(2)
     answers(1, din.at[0])
     ends(1)
     answers(2, din.at[1])
     ends(2)
+    chain(1, gx)
     relay_y(2).wait_recv()
     relay_x(2).wait_recv()
-    q_copy(0).start()
-    q_copy(1).start()
-    chain(1, gx)
     answers(3, din.at[2])
     ends(3)
     chain(2, gy)
@@ -376,9 +381,6 @@
     n_tok, width = tokens.shape
     hidden = gate_weight.shape[2]
     depth, cols, qcols = gate_weight.shape[1], down_weight.shape[2], query_weight.shape[1]
-    experts = jnp.arange(2 * NZ, dtype=jnp.int32)
-    named = routes[None, :, :] == experts[:, None, None]
-    gtab = jnp.sum(jnp.where(named, route_gain[None, :, :], 0.0), axis=2)
     n_rows = 2 * NZ * n_tok
     vmem = pl.BlockSpec(memory_space=pltpu.VMEM)
     b16, f32 = jnp.bfloat16, jnp.float32
@@ -389,10 +391,11 @@
             jax.ShapeDtypeStruct((n_tok, width), b16),
             jax.ShapeDtypeStruct((n_tok, 4 * qcols), b16),
         ),
-        in_specs=[vmem] * 7,
+        in_specs=[vmem] * 8,
         out_specs=(vmem, vmem),
         scratch_shapes=[
             pltpu.VMEM((n_rows, width), b16),
+            pltpu.VMEM((2 * NZ, n_tok), f32),
             pltpu.VMEM((2 * NZ, 2 * NZ, n_tok), f32),
             pltpu.VMEM((n_rows, n_tok), f32),
             pltpu.VMEM((3, depth, hidden), b16),
@@ -431,7 +434,7 @@
             collective_id=0, has_side_effects=True, vmem_limit_bytes=60 * 1024 * 1024
         ),
     )(
-        tokens, gtab, gate_weight[0], up_weight[0], down_weight[0],
+        tokens, routes.T, route_gain.T, gate_weight[0], up_weight[0], down_weight[0],
         norm_gain.reshape(1, width), query_weight,
     )
 

time: 144 us -> 149 us (1.035)
  Pallas kernels: 138 us -> 144 us
    pallas_call x1, Pallas kernels: 138 us -> 144 us  [fused(): pl.pallas_call(kernel, out_shape=(jax.ShapeDtypeStruct((n_tok, width), b1...]
where the time goes in v3:
time: 149 us
  Pallas kernels  144 us (97%)
  local copies, waits for them, and re-layouts  3.65 us (2%)
    pallas_call x1, Pallas kernels, fused(): pl.pallas_call(kernel, out_shape=(jax.ShapeDtypeStruct((n_tok, width), b1...  144 us
    unnamed x2, local copies, waits for them, and re-layouts  3.65 us

profile of v3, /device:TPU:0, one launch (start us, length us, event | category | flops | bytes accessed | tf_op | source)
XLA Modules:
  0.0 148.8 jit_solution(12512556515423682776)
XLA Ops:
  0.6 144.5 %shard_map.95 = (bf16[128,2048]{1,0:T(8,128)(2,1)}, bf16[128,1536]{1,0:T(8,128)(2,1)}) custom-call(bf16[128,2048]{1,0:T(8,128)(2,1)} %tok.1, s32[6,128]{1,0:T(8,128)} %bitcast.10, f32[6,128]{1,0:T(8,128)} %bitcast.11, bf16[512,768]{1,0:T(8,128)(2,1)} %bitcast.6, bf16[512,768]{1,0:T(8,128)(2,1)} %bitcast.7, bf16[768,512]{1,0:T(8,128)(2,1)} %bitcast.8, ...), custom_call_target="tpu_custom_call" | custom-call | tf_op jit(solution)/shard_map/pallas_call | solution.py:388
  145.1 1.9 %copy.12 = bf16[128,2048]{1,0:T(8,128)(2,1)} copy(bf16[128,2048]{1,0:T(8,128)(2,1)} %get-tuple-element.4) | data formatting | bytes 1048576
  147.0 1.8 %copy.13 = bf16[128,1536]{1,0:T(8,128)(2,1)} copy(bf16[128,1536]{1,0:T(8,128)(2,1)} %get-tuple-element.5) | data formatting | bytes 786432

commit v4 on v3

--- a/solution.py
+++ b/solution.py
@@ -145,8 +145,6 @@
     pass_on(0)
     hop(2)
     pass_on(1)
-    own_x(2).start()
-    own_y(2).start()
 
     for k in range(1, 2 * NZ):
         peer = (ep + k) % (2 * NZ)
@@ -182,6 +180,8 @@
     partial(acc_u, uin.at[1], gy, False)
     relay_y(0).wait_recv()
     relay_x(0).wait_recv()
+    own_x(2).start()
+    own_y(2).start()
     partial(acc_g, gin.at[2], gd, False)
     relay_y(1).wait_recv()
     relay_x(1).wait_recv()
@@ -240,26 +240,41 @@
                 rout[q, d] = (part[q, d] + sin[q, d].astype(jnp.float32)).astype(rout.dtype)
                 left_copy(q, d).start()
 
-    def chain(q, owner):
-        for k in range(NZ - 1):
-            d = NZ - 1 - k
-
-            @pl.when((z > 0) & (z < d))
-            def _():
-                right_copy(q, d).wait_recv()
-                rout[q, d] = (
-                    part[q, d] + sin[q, d].astype(jnp.float32) + rin[q, d].astype(jnp.float32)
-                ).astype(rout.dtype)
-                right_copy(q, d).start()
-
-            @pl.when((z < NZ - 1) & (z > k))
-            def _():
-                left_copy(q, k).wait_recv()
-                rout[q, k] = (
-                    part[q, k] + sin[q, k].astype(jnp.float32) + lin[q, k].astype(jnp.float32)
-                ).astype(rout.dtype)
-                left_copy(q, k).start()
-
+    def go_right(q, d):
+        right_copy(q, d).wait_recv()
+        rout[q, d] = (
+            part[q, d] + sin[q, d].astype(jnp.float32) + rin[q, d].astype(jnp.float32)
+        ).astype(rout.dtype)
+        right_copy(q, d).start()
+
+    def go_left(q, d):
+        left_copy(q, d).wait_recv()
+        rout[q, d] = (
+            part[q, d] + sin[q, d].astype(jnp.float32) + lin[q, d].astype(jnp.float32)
+        ).astype(rout.dtype)
+        left_copy(q, d).start()
+
+    def near(q):
+        @pl.when(z == 1)
+        def _():
+            for d in range(NZ - 1, 1, -1):
+                go_right(q, d)
+
+        @pl.when(z == NZ - 2)
+        def _():
+            for d in range(NZ - 2):
+                go_left(q, d)
+
+    def far(q):
+        @pl.when(z == NZ - 2)
+        def _():
+            go_right(q, NZ - 1)
+
+        @pl.when(z == 1)
+        def _():
+            go_left(q, 0)
+
+    def finish(q, owner):
         at = pl.ds(pl.multiple_of(owner * cols, cols), cols)
         total[:, at] = tok[:, at].astype(jnp.float32) + part[q, z] + sin[q, z].astype(jnp.float32)
 
@@ -302,26 +317,34 @@
     answers(0, dw)
     ends(0)
     pass_on(2)
+    near(0)
+    answers(1, din.at[0])
+    ends(1)
+    far(0)
+    answers(2, din.at[1])
+    ends(2)
+    near(1)
+    relay_y(2).wait_recv()
+    relay_x(2).wait_recv()
     q_copy(0).start()
     q_copy(1).start()
-    chain(0, g)
-    answers(1, din.at[0])
-    ends(1)
-    answers(2, din.at[1])
-    ends(2)
-    chain(1, gx)
-    relay_y(2).wait_recv()
-    relay_x(2).wait_recv()
     answers(3, din.at[2])
     ends(3)
-    chain(2, gy)
+    far(1)
+    near(2)
+    far(2)
+    near(3)
     q_copy(0).wait_recv()
     q_copy(2).start()
     q_copy(4).start()
     q_copy(1).wait_recv()
     q_copy(3).start()
     q_copy(5).start()
-    chain(3, gd)
+    far(3)
+    finish(0, g)
+    finish(1, gx)
+    finish(2, gy)
+    finish(3, gd)
 
     value = total[...]
     mixed[...] = value.astype(mixed.dtype)

time: 149 us -> 124 us (0.83)
  Pallas kernels: 144 us -> 118 us
    pallas_call x1, Pallas kernels: 144 us -> 118 us  [fused(): pl.pallas_call(kernel, out_shape=(jax.ShapeDtypeStruct((n_tok, width), b1...]
where the time goes in v4:
time: 124 us; the launch traced here: 123 us
  Pallas kernels  118 us (95%)
  local copies, waits for them, and re-layouts  3.65 us (3%)
    pallas_call x1, Pallas kernels, fused(): pl.pallas_call(kernel, out_shape=(jax.ShapeDtypeStruct((n_tok, width), b1...  118 us
    unnamed x2, local copies, waits for them, and re-layouts  3.65 us

profile of v4, /device:TPU:0, one launch (start us, length us, event | category | flops | bytes accessed | tf_op | source)
XLA Modules:
  0.0 122.7 jit_solution(12480144072077825649)
XLA Ops:
  0.6 118.4 %shard_map.95 = (bf16[128,2048]{1,0:T(8,128)(2,1)}, bf16[128,1536]{1,0:T(8,128)(2,1)}) custom-call(bf16[128,2048]{1,0:T(8,128)(2,1)} %tok.1, s32[6,128]{1,0:T(8,128)} %bitcast.10, f32[6,128]{1,0:T(8,128)} %bitcast.11, bf16[512,768]{1,0:T(8,128)(2,1)} %bitcast.6, bf16[512,768]{1,0:T(8,128)(2,1)} %bitcast.7, bf16[768,512]{1,0:T(8,128)(2,1)} %bitcast.8, ...), custom_call_target="tpu_custom_call" | custom-call | tf_op jit(solution)/shard_map/pallas_call | solution.py:411
  119.0 1.9 %copy.12 = bf16[128,2048]{1,0:T(8,128)(2,1)} copy(bf16[128,2048]{1,0:T(8,128)(2,1)} %get-tuple-element.4) | data formatting | bytes 1048576
  120.9 1.8 %copy.13 = bf16[128,1536]{1,0:T(8,128)(2,1)} copy(bf16[128,1536]{1,0:T(8,128)(2,1)} %get-tuple-element.5) | data formatting | bytes 786432

commit v5 on v4

--- a/solution.py
+++ b/solution.py
@@ -10,11 +10,12 @@
 
 
 def kernel(
-    tok, routes, gain, gw, uw, dw, ng, qw, mixed, query,
+    tok, routes, gain, gw_far, uw_far, dw_far, ng, qw_far, mixed, query,
+    gw, uw, dw, qw,
     rows, gtab, gains, scale, gin, uin, din, qin, acc_g, acc_u, hid,
     sout, sin, part, rin, lin, rout, total, normed,
     gain_s, gain_r, tok_r, tok_sr, tok_sl, tok_ss, w_s, w_r, q_s, q_r,
-    sib_s, sib_r, right_s, right_r, left_s, left_r,
+    sib_s, sib_r, right_s, right_r, left_s, left_r, own_r,
 ):
     g = lax.axis_index("grp")
     ep = lax.axis_index("ep")
@@ -64,7 +65,7 @@
 
     tok_copy(tok, z, tok_ss, sib).start()
 
-    shards_of = ((gw, gin), (uw, uin), (dw, din))
+    shards_of = ((gw_far, gin), (uw_far, uin), (dw_far, din))
 
     def own_x(i):
         src, dst = shards_of[i]
@@ -94,6 +95,13 @@
     own_x(1).start()
     own_y(1).start()
 
+    def fetch(i):
+        src, dst = ((gw_far, gw), (uw_far, uw), (dw_far, dw), (qw_far, qw))[i]
+        return pltpu.make_async_copy(src, dst, own_r.at[i])
+
+    for i in range(4):
+        fetch(i).start()
+
     def gain_copy(k):
         return remote(
             gtab, gains.at[c * NZ + z], gain_s.at[k], gain_r.at[c * NZ + z],
@@ -140,7 +148,32 @@
         own_y(i).wait_recv()
         relay_x(i).start()
 
+    tile = 2 * n_tok
+    tiles = rows.shape[0] // tile
+    half_line = NZ // 2
+    mine = z // half_line
+
+    def partial_tile(acc, w, owner, first, i):
+        at = pl.ds(pl.multiple_of(owner * depth, depth), depth)
+        r = pl.ds(pl.multiple_of(i * tile, tile), tile)
+        p = jnp.dot(rows[r, at], w[...], preferred_element_type=jnp.float32)
+        acc[r, :] = p if first else acc[r, :] + p
+
+    def own_tiles(line_half):
+        def body(cc, carry):
+            i = cc * half_line + line_half
+            partial_tile(acc_g, gw, g, True, i)
+            partial_tile(acc_u, uw, g, True, i)
+            return carry
+
+        lax.fori_loop(0, 2, body, 0)
+
     hop(0)
+    fetch(0).wait()
+    fetch(1).wait()
+    for k in range(half_line):
+        tok_wait(mine * half_line + k, 1 - c)
+    own_tiles(mine)
     hop(1)
     pass_on(0)
     hop(2)
@@ -155,25 +188,17 @@
         chosen = lax.broadcasted_iota(jnp.int32, table.shape, 0) == ep
         line = jnp.sum(jnp.where(chosen, table, 0.0), axis=0, keepdims=True)
         scale[b * n_tok : (b + 1) * n_tok, :] = jnp.broadcast_to(line, (n_tok, n_tok)).T
-    for zz in range(NZ):
-        tok_wait(zz, 1 - c)
-
-    tile = 2 * n_tok
-    tiles = rows.shape[0] // tile
+    for k in range(half_line):
+        tok_wait((1 - mine) * half_line + k, 1 - c)
 
     def partial(acc, w, owner, first):
-        at = pl.ds(pl.multiple_of(owner * depth, depth), depth)
-
         def body(i, carry):
-            r = pl.ds(pl.multiple_of(i * tile, tile), tile)
-            p = jnp.dot(rows[r, at], w[...], preferred_element_type=jnp.float32)
-            acc[r, :] = p if first else acc[r, :] + p
+            partial_tile(acc, w, owner, first, i)
             return carry
 
         lax.fori_loop(0, tiles, body, 0)
 
-    partial(acc_g, gw, g, True)
-    partial(acc_u, uw, g, True)
+    own_tiles(1 - mine)
     partial(acc_g, gin.at[0], gx, False)
     partial(acc_g, gin.at[1], gy, False)
     partial(acc_u, uin.at[0], gx, False)
@@ -296,9 +321,9 @@
 
     def q_copy(k):
         if k == 0:
-            return remote(qw.at[half_at], qin.at[0, half_at], q_s.at[0], q_r.at[0], x_dev)
+            return remote(qw_far.at[half_at], qin.at[0, half_at], q_s.at[0], q_r.at[0], x_dev)
         if k == 1:
-            return remote(qw.at[half_at], qin.at[1, half_at], q_s.at[1], q_r.at[1], y_dev)
+            return remote(qw_far.at[half_at], qin.at[1, half_at], q_s.at[1], q_r.at[1], y_dev)
         if k == 2:
             return remote(qin.at[0, first_at], qin.at[2, first_at], q_s.at[2], q_r.at[2], y_dev)
         if k == 3:
@@ -314,6 +339,7 @@
         slot, at = ((0, other_half), (1, other_half), (2, other_first), (2, other_second))[k - 4]
         remote(qin.at[slot, at], qin.at[slot, at], q_s.at[k], q_r.at[k], sib).wait_recv()
 
+    fetch(2).wait()
     answers(0, dw)
     ends(0)
     pass_on(2)
@@ -334,6 +360,8 @@
     near(2)
     far(2)
     near(3)
+    finish(0, g)
+    finish(1, gx)
     q_copy(0).wait_recv()
     q_copy(2).start()
     q_copy(4).start()
@@ -341,8 +369,6 @@
     q_copy(3).start()
     q_copy(5).start()
     far(3)
-    finish(0, g)
-    finish(1, gx)
     finish(2, gy)
     finish(3, gd)
 
@@ -357,6 +383,7 @@
             normed[...], w[...], preferred_element_type=jnp.float32
         ).astype(query.dtype)
 
+    fetch(3).wait()
     project(qw, g)
     q_wait_sib(4)
     project(qin.at[0], gx)
@@ -406,6 +433,7 @@
     depth, cols, qcols = gate_weight.shape[1], down_weight.shape[2], query_weight.shape[1]
     n_rows = 2 * NZ * n_tok
     vmem = pl.BlockSpec(memory_space=pltpu.VMEM)
+    hbm = pl.BlockSpec(memory_space=pl.ANY)
     b16, f32 = jnp.bfloat16, jnp.float32
     dma = pltpu.SemaphoreType.DMA
     return pl.pallas_call(
@@ -414,9 +442,13 @@
             jax.ShapeDtypeStruct((n_tok, width), b16),
             jax.ShapeDtypeStruct((n_tok, 4 * qcols), b16),
         ),
-        in_specs=[vmem] * 8,
+        in_specs=[vmem] * 3 + [hbm] * 3 + [vmem, hbm],
         out_specs=(vmem, vmem),
         scratch_shapes=[
+            pltpu.VMEM((depth, hidden), b16),
+            pltpu.VMEM((depth, hidden), b16),
+            pltpu.VMEM((hidden, cols), b16),
+            pltpu.VMEM((width, qcols), b16),
             pltpu.VMEM((n_rows, width), b16),
             pltpu.VMEM((2 * NZ, n_tok), f32),
             pltpu.VMEM((2 * NZ, 2 * NZ, n_tok), f32),
@@ -452,6 +484,7 @@
             dma((4, NZ)),
             dma((4, NZ)),
             dma((4, NZ)),
+            dma((4,)),
         ],
         compiler_params=pltpu.CompilerParams(
             collective_id=0, has_side_effects=True, vmem_limit_bytes=60 * 1024 * 1024

time: 124 us -> 123 us (level)
  no operation moved by 1% of the time
where the time goes in v5:
time: 123 us; the launch traced here: 122 us
  Pallas kernels  118 us (96%)
  local copies, waits for them, and re-layouts  3.65 us (3%)
    pallas_call x1, Pallas kernels, fused(): pl.pallas_call(kernel, out_shape=(jax.ShapeDtypeStruct((n_tok, width), b1...  118 us
    unnamed x2, local copies, waits for them, and re-layouts  3.65 us

profile of v5, /device:TPU:0, one launch (start us, length us, event | category | flops | bytes accessed | tf_op | source)
XLA Modules:
  0.0 121.9 jit_solution(13531559724288339979)
XLA Ops:
  0.6 117.6 %shard_map.95 = (bf16[128,2048]{1,0:T(8,128)(2,1)}, bf16[128,1536]{1,0:T(8,128)(2,1)}) custom-call(bf16[128,2048]{1,0:T(8,128)(2,1)} %tok.1, s32[6,128]{1,0:T(8,128)} %bitcast.10, f32[6,128]{1,0:T(8,128)} %bitcast.11, bf16[512,768]{1,0:T(8,128)(2,1)} %bitcast.6, bf16[512,768]{1,0:T(8,128)(2,1)} %bitcast.7, bf16[768,512]{1,0:T(8,128)(2,1)} %bitcast.8, ...), custom_call_target="tpu_custom_call" | custom-call | tf_op jit(solution)/shard_map/pallas_call | solution.py:439
  118.2 1.9 %copy.12 = bf16[128,2048]{1,0:T(8,128)(2,1)} copy(bf16[128,2048]{1,0:T(8,128)(2,1)} %get-tuple-element.4) | data formatting | bytes 1048576
  120.1 1.8 %copy.13 = bf16[128,1536]{1,0:T(8,128)(2,1)} copy(bf16[128,1536]{1,0:T(8,128)(2,1)} %get-tuple-element.5) | data formatting | bytes 786432
